TPU v7x, 32 devices: a whole 2x2x4 slice. The times are simulated.
32 devices in a mesh: ctx: 8 (over y, x, core), ch: 4 (over z).
Axes of the slice: x: 2, y: 2, z: 4, core: 2. Of those that a mesh axis runs over, the one named last changes fastest.
Arguments:
- stream: bfloat16 [4096, 4096], P('ctx', 'ch'), may hold values from -900 to 900
- key_gate: bfloat16 [4096, 4096], P('ctx', 'ch'), may hold values from -6 to 6
- query_gate: bfloat16 [4096, 4096], P('ctx', 'ch'), may hold values from -6 to 6
- grad_output: bfloat16 [4096, 4096], P('ctx', 'ch'), may hold values from -50 to 50
- norm_gain: float32 [4096], P('ch'), may hold values from 0.1 to 1.9
- residue: float32 [4096, 16], P('ch'), may hold values from -0.5 to 0.5
- log_rate: float32 [4096, 16], P('ch'), may hold values from -14 to -2.9
Outputs:
- output: bfloat16 [4096, 4096], P('ctx', 'ch')
- grad_stream: bfloat16 [4096, 4096], P('ctx', 'ch')
- grad_key: bfloat16 [4096, 4096], P('ctx', 'ch')
- grad_query: bfloat16 [4096, 4096], P('ctx', 'ch')
- grad_gain: float32 [4096], P('ch')
- grad_residue: float32 [4096, 16], P('ch')
- grad_rate: float32 [4096, 16], P('ch')
All inputs are finite; a program needn't handle non-finite values.
Results may differ from a plain program's by a relative error of at most 0.008.
Values sent between devices are 32-bit elements; how exact they have to be, the bound alone decides.
A program may use at most 128 MiB of HBM per device.

v0:
```python
import functools
import math

import jax
import jax.numpy as jnp
from jax import lax
from jax.experimental import pallas as pl
from jax.experimental.pallas import tpu as pltpu
from jax.sharding import PartitionSpec as P

D = 4096
MODES = 16
epsilon = 1e-05
LANES = 128
RB = 16
UNROLL = 8
GROUP = 8
MESH = pl.DeviceIdType.MESH
F32 = jnp.float32


def kernel(
    n, nch, rows, kt,
    stream, key, query, gout, gain, res, lrate,
    out, gstream, gkey, gquery, ggain, gres, grate,
    xs, gs, ys, ss, qbuf, apow, alen, col, inv_col, in_row, nrm_buf, inner_buf,
    sbuf, tbuf, state, part, rsbuf, agbuf, gainbuf,
    nrm_s, nrm_r, inner_s, inner_r, s_s, s_r, t_s, t_r, rs_s, rs_r, ag_s, ag_r, gn_s, gn_r,
):
    me = lax.axis_index("ctx")
    mc = lax.axis_index("ch")
    nblk = rows // RB
    nstep = rows // UNROLL
    per = 2 * MODES // n

    def each(count, test, fn):
        def body(j, carry):
            @pl.when(test(j))
            def _():
                fn(j)

            return carry

        lax.fori_loop(0, count, body, 0)

    def remote(src, dst, ssem, rsem, axis, j):
        return pltpu.make_async_remote_copy(
            src_ref=src, dst_ref=dst, send_sem=ssem, recv_sem=rsem,
            device_id={axis: j}, device_id_type=MESH,
        )

    def c_nrm(j):
        return remote(nrm_buf.at[mc], nrm_buf.at[mc], nrm_s.at[j], nrm_r.at[mc], "ch", j)

    def w_nrm(j):
        return remote(nrm_buf.at[j], nrm_buf.at[j], nrm_s.at[j], nrm_r.at[j], "ch", j)

    def c_inner(j):
        return remote(inner_buf.at[mc], inner_buf.at[mc], inner_s.at[j], inner_r.at[mc], "ch", j)

    def w_inner(j):
        return remote(inner_buf.at[j], inner_buf.at[j], inner_s.at[j], inner_r.at[j], "ch", j)

    def c_s(j):
        return remote(sbuf.at[me], sbuf.at[me], s_s.at[j], s_r.at[me], "ctx", j)

    def w_s(j):
        return remote(sbuf.at[j], sbuf.at[j], s_s.at[j], s_r.at[j], "ctx", j)

    def c_t(j):
        return remote(tbuf.at[me], tbuf.at[me], t_s.at[j], t_r.at[me], "ctx", j)

    def w_t(j):
        return remote(tbuf.at[j], tbuf.at[j], t_s.at[j], t_r.at[j], "ctx", j)

    def c_rs(j):
        return remote(part.at[pl.ds(j * per, per)], rsbuf.at[me], rs_s.at[j], rs_r.at[me], "ctx", j)

    def w_rs(j):
        return remote(rsbuf.at[j], rsbuf.at[j], rs_s.at[j], rs_r.at[j], "ctx", j)

    def c_ag(j):
        return remote(agbuf.at[me], agbuf.at[me], ag_s.at[j], ag_r.at[me], "ctx", j)

    def w_ag(j):
        return remote(agbuf.at[j], agbuf.at[j], ag_s.at[j], ag_r.at[j], "ctx", j)

    def c_gn(j):
        return remote(gainbuf.at[me], gainbuf.at[me], gn_s.at[j], gn_r.at[me], "ctx", j)

    def w_gn(j):
        return remote(gainbuf.at[j], gainbuf.at[j], gn_s.at[j], gn_r.at[j], "ctx", j)

    barrier = pltpu.get_barrier_semaphore()
    each(n, lambda j: j != me, lambda j: pl.semaphore_signal(
        barrier, inc=1, device_id={"ctx": j}, device_id_type=MESH))
    each(nch, lambda j: j != mc, lambda j: pl.semaphore_signal(
        barrier, inc=1, device_id={"ch": j}, device_id_type=MESH))

    rate = jnp.exp(lrate[...])
    apow[...] = jnp.exp(-rate)
    alen[...] = jnp.exp(-rate * float(rows))

    def lanes(k):
        return pl.ds(k * LANES, LANES)

    def rows_of(b):
        return pl.ds(pl.multiple_of(b * RB, RB), RB)

    def spread(b, k):
        return pl.ds(b * (RB * kt) + k, RB, stride=kt)

    def at(t):
        return pl.ds(pl.multiple_of(t * kt, kt), kt)

    def to_row(ref):
        return jnp.broadcast_to(jnp.sum(ref[...].T, axis=0, keepdims=True), (8, rows))

    def first(b, carry):
        r = rows_of(b)
        total = jnp.zeros((RB, LANES), F32)
        for k in range(kt):
            s = stream[r, lanes(k)].astype(F32)
            total += s * s
            gs[spread(b, k), :] = gout[r, lanes(k)].astype(F32) * query[r, lanes(k)].astype(F32)
        col[r, :] = total
        return carry

    lax.fori_loop(0, nblk, first, 0)
    nrm_buf[mc] = to_row(col)
    pl.semaphore_wait(barrier, n - 1 + nch - 1)
    each(nch, lambda j: j != mc, lambda j: c_nrm(j).start())

    def end_state(src, backward):
        a = [apow[m] for m in range(MODES)]

        def body(i, carry):
            h = list(carry)
            for u in range(UNROLL):
                t = i * UNROLL + u
                x = src[at(rows - 1 - t if backward else t), :]
                for m in range(MODES):
                    h[m] = a[m] * h[m] + x
            return tuple(h)

        zero = jnp.zeros((kt, LANES), F32)
        return lax.fori_loop(0, nstep, body, (zero,) * MODES)

    ends = end_state(gs, True)
    for m in range(MODES):
        tbuf[me, m] = ends[m]
    each(n, lambda j: j < me, lambda j: c_t(j).start())

    each(nch, lambda j: j != mc, lambda j: w_nrm(j).wait_recv())
    total = nrm_buf[0]
    for j in range(1, nch):
        total = total + nrm_buf[j]
    inv_row = lax.rsqrt(total / D + epsilon)
    inv_col[...] = jnp.broadcast_to(inv_row[0:1], (LANES, rows)).T

    def second(b, carry):
        r = rows_of(b)
        iv = inv_col[r, :]
        for k in range(kt):
            normed = stream[r, lanes(k)].astype(F32) * iv * gain[k : k + 1, :]
            x = (key[r, lanes(k)].astype(F32) * normed).astype(jnp.bfloat16)
            xs[spread(b, k), :] = x.astype(F32)
        return carry

    lax.fori_loop(0, nblk, second, 0)
    ends = end_state(xs, False)
    for m in range(MODES):
        sbuf[me, m] = ends[m]
    each(n, lambda j: j > me, lambda j: c_s(j).start())

    def backward(group):
        m0 = group * GROUP
        a = [apow[m0 + m] for m in range(GROUP)]
        c = [res[m0 + m] for m in range(GROUP)]

        def body(i, carry):
            q = list(carry)
            for u in range(UNROLL):
                t = rows - 1 - (i * UNROLL + u)
                g = gs[at(t), :]
                acc = ss[at(t), :] if group else None
                for m in range(GROUP):
                    q[m] = a[m] * q[m] + g
                    qbuf[t, m] = q[m]
                    term = c[m] * q[m]
                    acc = term if acc is None else acc + term
                ss[at(t), :] = acc
            return tuple(q)

        lax.fori_loop(0, nstep, body, tuple(state[1, m0 + m] for m in range(GROUP)))

    def forward(group):
        m0 = group * GROUP
        a = [apow[m0 + m] for m in range(GROUP)]
        c = [res[m0 + m] for m in range(GROUP)]
        zero = jnp.zeros((kt, LANES), F32)

        def body(i, carry):
            h, gr, gw = (list(v) for v in carry)
            for u in range(UNROLL):
                t = i * UNROLL + u
                x = xs[at(t), :]
                g = gs[at(t), :]
                acc = ys[at(t), :] if group else None
                for m in range(GROUP):
                    z = a[m] * h[m]
                    gw[m] = gw[m] + z * qbuf[t, m]
                    h[m] = z + x
                    gr[m] = gr[m] + g * h[m]
                    term = c[m] * h[m]
                    acc = term if acc is None else acc + term
                ys[at(t), :] = acc
            return tuple(h), tuple(gr), tuple(gw)

        start = tuple(state[0, m0 + m] for m in range(GROUP))
        unused, gr, gw = lax.fori_loop(0, nstep, body, (start, (zero,) * GROUP, (zero,) * GROUP))
        for m in range(GROUP):
            part[m0 + m] = gr[m]
            part[MODES + m0 + m] = gw[m]

    state[...] = jnp.zeros_like(state)

    def take_t(i):
        j = n - 1 - i
        w_t(j).wait_recv()
        state[1] = alen[...] * state[1] + tbuf[j]

    each(n, lambda i: n - 1 - i > me, take_t)
    backward(0)

    def take_s(j):
        w_s(j).wait_recv()
        state[0] = alen[...] * state[0] + sbuf[j]

    each(n, lambda j: j < me, take_s)
    forward(0)
    for group in range(1, MODES // GROUP - 1):
        backward(group)
        forward(group)
    backward(MODES // GROUP - 1)

    def third(b, carry):
        r = rows_of(b)
        iv = inv_col[r, :]
        total = jnp.zeros((RB, LANES), F32)
        gains = list(carry)
        for k in range(kt):
            unit = stream[r, lanes(k)].astype(F32) * iv
            gk = gain[k : k + 1, :]
            sig = ss[spread(b, k), :]
            gkey[r, lanes(k)] = (sig * (unit * gk)).astype(jnp.bfloat16)
            prod = sig * key[r, lanes(k)].astype(F32) * unit
            gains[k] = gains[k] + prod
            total += prod * gk
        col[r, :] = total
        return tuple(gains)

    gains = lax.fori_loop(0, nblk, third, (jnp.zeros((RB, LANES), F32),) * kt)
    for k in range(kt):
        gainbuf[me, k : k + 1, :] = jnp.sum(gains[k], axis=0, keepdims=True)
    inner_buf[mc] = to_row(col)
    each(nch, lambda j: j != mc, lambda j: c_inner(j).start())
    each(n, lambda j: j != me, lambda j: c_gn(j).start())

    forward(MODES // GROUP - 1)
    rsbuf[me] = part[pl.ds(me * per, per)]
    each(n, lambda j: j != me, lambda j: c_rs(j).start())

    def fourth(b, carry):
        r = rows_of(b)
        for k in range(kt):
            conv = ys[spread(b, k), :]
            out[r, lanes(k)] = (query[r, lanes(k)].astype(F32) * conv).astype(jnp.bfloat16)
            gquery[r, lanes(k)] = (gout[r, lanes(k)].astype(F32) * conv).astype(jnp.bfloat16)
        return carry

    lax.fori_loop(0, nblk, fourth, 0)

    each(n, lambda j: j != me, lambda j: w_rs(j).wait_recv())
    agbuf[me] = lax.fori_loop(
        1, n, lambda j, acc: acc + rsbuf[j], rsbuf[0])
    each(n, lambda j: j != me, lambda j: c_ag(j).start())

    each(nch, lambda j: j != mc, lambda j: w_inner(j).wait_recv())
    total = inner_buf[0]
    for j in range(1, nch):
        total = total + inner_buf[j]
    col[...] = jnp.broadcast_to((total / D)[0:1], (LANES, rows)).T

    def fifth(b, carry):
        r = rows_of(b)
        iv = inv_col[r, :]
        inner = col[r, :]
        for k in range(kt):
            unit = stream[r, lanes(k)].astype(F32) * iv
            unit_grad = ss[spread(b, k), :] * key[r, lanes(k)].astype(F32) * gain[k : k + 1, :]
            gstream[r, lanes(k)] = (iv * (unit_grad - unit * inner)).astype(jnp.bfloat16)
        return carry

    lax.fori_loop(0, nblk, fifth, 0)

    scale = 1.0 / math.sqrt(rows * n)
    each(n, lambda j: j != me, lambda j: w_gn(j).wait_recv())
    ggain[...] = lax.fori_loop(1, n, lambda j, acc: acc + gainbuf[j], gainbuf[0]) * scale
    each(n, lambda j: j != me, lambda j: w_ag(j).wait_recv())
    for m in range(MODES):
        gres[m] = agbuf[m // per, m % per] * scale
        w = MODES + m
        grate[m] = -jnp.exp(lrate[m]) * res[m] * (agbuf[w // per, w % per] * scale)

    each(nch, lambda j: j != mc, lambda j: c_nrm(j).wait_send())
    each(nch, lambda j: j != mc, lambda j: c_inner(j).wait_send())
    each(n, lambda j: j < me, lambda j: c_t(j).wait_send())
    each(n, lambda j: j > me, lambda j: c_s(j).wait_send())
    each(n, lambda j: j != me, lambda j: c_gn(j).wait_send())
    each(n, lambda j: j != me, lambda j: c_rs(j).wait_send())
    each(n, lambda j: j != me, lambda j: c_ag(j).wait_send())


def local(n, nch, stream, key_gate, query_gate, grad_output, norm_gain, residue, log_rate):
    rows, channels = stream.shape
    kt = channels // LANES
    per = 2 * MODES // n
    vm = pl.BlockSpec(memory_space=pltpu.VMEM)
    wide = jax.ShapeDtypeStruct((rows, channels), jnp.bfloat16)
    modal = jax.ShapeDtypeStruct((MODES, kt, LANES), F32)
    dma = pltpu.SemaphoreType.DMA
    flat = pltpu.VMEM((rows * kt, LANES), F32)
    one = pltpu.VMEM((rows, LANES), F32)
    lined = pltpu.VMEM((nch, 8, rows), F32)
    ends = pltpu.VMEM((n, MODES, kt, LANES), F32)
    mode = pltpu.VMEM((MODES, kt, LANES), F32)
    pieces = pltpu.VMEM((n, per, kt, LANES), F32)
    out, gstream, gkey, gquery, ggain, gres, grate = pl.pallas_call(
        functools.partial(kernel, n, nch, rows, kt),
        out_shape=(wide, wide, wide, wide, jax.ShapeDtypeStruct((kt, LANES), F32), modal, modal),
        in_specs=[vm] * 7,
        out_specs=(vm,) * 7,
        scratch_shapes=[
            flat, flat, flat, flat,
            pltpu.VMEM((rows, GROUP, kt, LANES), F32),
            mode, mode, one, one,
            pltpu.VMEM((8, rows), F32),
            lined, lined, ends, ends,
            pltpu.VMEM((2, MODES, kt, LANES), F32),
            pltpu.VMEM((2 * MODES, kt, LANES), F32),
            pieces, pieces,
            pltpu.VMEM((n, kt, LANES), F32),
            dma((nch,)), dma((nch,)), dma((nch,)), dma((nch,)),
        ] + [dma((n,))] * 10,
        compiler_params=pltpu.CompilerParams(
            collective_id=0, has_side_effects=True, vmem_limit_bytes=56 * 2**20
        ),
    )(
        stream, key_gate, query_gate, grad_output,
        norm_gain.reshape(kt, LANES),
        residue.T.reshape(MODES, kt, LANES),
        log_rate.T.reshape(MODES, kt, LANES),
    )
    return (
        out, gstream, gkey, gquery, ggain.reshape(channels),
        gres.reshape(MODES, channels).T, grate.reshape(MODES, channels).T,
    )


def solution(mesh):
    wide = P("ctx", "ch")
    thin = P("ch", None)
    return jax.shard_map(
        functools.partial(local, mesh.shape["ctx"], mesh.shape["ch"]),
        mesh=mesh,
        in_specs=(wide, wide, wide, wide, P("ch"), thin, thin),
        out_specs=(wide, wide, wide, wide, P("ch"), thin, thin),
        check_vma=False,
    )
```

profile of v0, /device:TPU:0, one launch (start us, length us, event | category | flops | bytes accessed | tf_op | source)
XLA Modules:
  0.0 58.6 jit_solution(647053722492001492)
XLA Ops:
  0.6 0.0 copy-start.3
  0.6 1.5 %copy.14 = f32[2,8,8,128]{3,2,1,0:T(8,128)} copy(f32[2,8,8,128]{3,1,2,0:T(8,128)} %bitcast.20) | data formatting | bytes 131072
  2.2 0.0 copy-done.3
  2.2 0.6 %copy.15 = f32[2,8,8,128]{3,2,1,0:T(8,128)} copy(f32[2,8,8,128]{3,1,2,0:T(8,128)S(1)} %bitcast.21) | data formatting | bytes 131072
  2.8 47.1 %shard_map.126 = (bf16[512,1024]{1,0:T(8,128)(2,1)}, bf16[512,1024]{1,0:T(8,128)(2,1)}, bf16[512,1024]{1,0:T(8,128)(2,1)}, bf16[512,1024]{1,0:T(8,128)(2,1)}, f3...) custom-call(bf16[512,1024]{1,0:T(8,128)(2,1)} %stream.1, bf16[512,1024]{1,0:T(8,128)(2,1)} %key.1, ...), custom_call_target="tpu_custom_call" | custom-call | tf_op jit(solution)/shard_map/pallas_call | solution.py:339
  49.9 1.5 %bitcast_bitcast_fusion = (f32[1024,16]{0,1:T(8,128)}, f32[1024,16]{0,1:T(8,128)}) fusion(f32[2,8,8,128]{3,2,1,0:T(8,128)} %bitcast.23, f32[2,8,8,128]{3,2,1,0:T(8,128)} %bitcast.22), kind=kLoop, calls=%fused_computation | loop fusion | bytes 262144 | tf_op jit(solution)/shard_map/transpose | solution.py:367
  51.5 0.0 copy-start.2
  51.5 2.4 %copy.25 = bf16[512,1024]{1,0:T(8,128)(2,1)} copy(bf16[512,1024]{1,0:T(8,128)(2,1)} %get-tuple-element.30) | data formatting | bytes 2097152
  53.8 0.0 copy-done.2
  53.8 0.0 copy-start.1
  53.8 1.0 %copy.26 = bf16[512,1024]{1,0:T(8,128)(2,1)} copy(bf16[512,1024]{1,0:T(8,128)(2,1)S(1)} %copy-done.2) | data formatting | bytes 2097152
  54.8 0.6 %copy-done.1 = bf16[512,1024]{1,0:T(8,128)(2,1)S(1)} copy-done((bf16[512,1024]{1,0:T(8,128)(2,1)S(1)}, bf16[512,1024]{1,0:T(8,128)(2,1)}, u32[]{:S(2)}) %copy-start.1) | copy-done | bytes 1048600
  55.4 0.0 copy-start
  55.4 1.0 %copy.27 = bf16[512,1024]{1,0:T(8,128)(2,1)} copy(bf16[512,1024]{1,0:T(8,128)(2,1)S(1)} %copy-done.1) | data formatting | bytes 2097152
  56.4 0.6 %copy-done = bf16[512,1024]{1,0:T(8,128)(2,1)S(1)} copy-done((bf16[512,1024]{1,0:T(8,128)(2,1)S(1)}, bf16[512,1024]{1,0:T(8,128)(2,1)}, u32[]{:S(2)}) %copy-start) | copy-done | bytes 1048600
  57.1 0.0 copy-start.4
  57.1 1.0 %copy.28 = bf16[512,1024]{1,0:T(8,128)(2,1)} copy(bf16[512,1024]{1,0:T(8,128)(2,1)S(1)} %copy-done) | data formatting | bytes 2097152
  58.0 0.0 copy-done.4
  58.0 0.6 %copy.29 = f32[1024]{0:T(1024)} copy(f32[1024]{0:T(1024)S(1)} %bitcast.25) | data formatting | bytes 8192
Async XLA Ops:
  0.6 1.5 %copy-start.3 = (f32[1024,16]{0,1:T(8,128)S(1)}, f32[1024,16]{0,1:T(8,128)}, u32[]{:S(2)}) copy-start(f32[1024,16]{0,1:T(8,128)} %param.13) | copy-start | bytes 196612
  51.5 2.4 %copy-start.2 = (bf16[512,1024]{1,0:T(8,128)(2,1)S(1)}, bf16[512,1024]{1,0:T(8,128)(2,1)}, u32[]{:S(2)}) copy-start(bf16[512,1024]{1,0:T(8,128)(2,1)} %get-tuple-element.31) | copy-start | bytes 3145732
  53.8 1.6 %copy-start.1 = (bf16[512,1024]{1,0:T(8,128)(2,1)S(1)}, bf16[512,1024]{1,0:T(8,128)(2,1)}, u32[]{:S(2)}) copy-start(bf16[512,1024]{1,0:T(8,128)(2,1)} %get-tuple-element.32) | copy-start | bytes 3145732
  55.4 1.6 %copy-start = (bf16[512,1024]{1,0:T(8,128)(2,1)S(1)}, bf16[512,1024]{1,0:T(8,128)(2,1)}, u32[]{:S(2)}) copy-start(bf16[512,1024]{1,0:T(8,128)(2,1)} %get-tuple-element.33) | copy-start | bytes 3145732
  57.1 1.0 %copy-start.4 = (f32[8,128]{1,0:T(8,128)S(1)}, f32[8,128]{1,0:T(8,128)}, u32[]{:S(2)}) copy-start(f32[8,128]{1,0:T(8,128)} %get-tuple-element.18) | copy-start | bytes 12292
where the time goes:
time: 59 us; the launch traced here: 58.6 us
  Pallas kernels  47.1 us (80%)
  local copies, waits for them, and re-layouts  10.8 us (18%)
  between operations  0.66 us (1%)
    pallas_call x1, Pallas kernels, local(): pl.pallas_call(functools.partial(kernel, n, nch, rows, kt), out_shape=(wi...  47.1 us
    unnamed x17, local copies, waits for them, and re-layouts  9.29 us
    transpose x1, local copies, waits for them, and re-layouts, local(): grate.reshape(MODES, channels)  1.54 us

commit v1 on v0

v1 whole, which is shorter than its diff:
```python
import functools
import math

import jax
import jax.numpy as jnp
from jax import lax
from jax.experimental import pallas as pl
from jax.experimental.pallas import tpu as pltpu
from jax.sharding import PartitionSpec as P

D = 4096
MODES = 16
epsilon = 1e-05
LANES = 128
RB = 16
UNROLL = 8
GROUP = 8
MESH = pl.DeviceIdType.MESH
F32 = jnp.float32


def kernel(
    n, nch, rows, kt,
    stream_in, key_in, query_in, gout_in, gain, res_in, lrate_in,
    conv_out, sig_out, inv_out, inner_out, ggain, gmode,
    stream, key, query, gout, xs, gs, ys, ss, qbuf, res, lrate, apow, alen,
    col, inv_col, nrm_buf, inner_buf, io_s,
    sbuf, tbuf, state, part, rsbuf, agbuf, gainbuf,
    nrm_s, nrm_r, inner_s, inner_r, s_s, s_r, t_s, t_r, rs_s, rs_r, ag_s, ag_r, gn_s, gn_r,
):
    me = lax.axis_index("ctx")
    mc = lax.axis_index("ch")
    nblk = rows // RB
    nstep = rows // UNROLL
    per = 2 * MODES // n

    def each(count, test, fn):
        def body(j, carry):
            @pl.when(test(j))
            def _():
                fn(j)

            return carry

        lax.fori_loop(0, count, body, 0)

    def remote(src, dst, ssem, rsem, axis, j):
        return pltpu.make_async_remote_copy(
            src_ref=src, dst_ref=dst, send_sem=ssem, recv_sem=rsem,
            device_id={axis: j}, device_id_type=MESH,
        )

    def c_nrm(j):
        return remote(nrm_buf.at[mc], nrm_buf.at[mc], nrm_s.at[j], nrm_r.at[mc], "ch", j)

    def w_nrm(j):
        return remote(nrm_buf.at[j], nrm_buf.at[j], nrm_s.at[j], nrm_r.at[j], "ch", j)

    def c_inner(j):
        return remote(inner_buf.at[mc], inner_buf.at[mc], inner_s.at[j], inner_r.at[mc], "ch", j)

    def w_inner(j):
        return remote(inner_buf.at[j], inner_buf.at[j], inner_s.at[j], inner_r.at[j], "ch", j)

    def c_s(j):
        return remote(sbuf.at[me], sbuf.at[me], s_s.at[j], s_r.at[me], "ctx", j)

    def w_s(j):
        return remote(sbuf.at[j], sbuf.at[j], s_s.at[j], s_r.at[j], "ctx", j)

    def c_t(j):
        return remote(tbuf.at[me], tbuf.at[me], t_s.at[j], t_r.at[me], "ctx", j)

    def w_t(j):
        return remote(tbuf.at[j], tbuf.at[j], t_s.at[j], t_r.at[j], "ctx", j)

    def c_rs(j):
        return remote(part.at[pl.ds(j * per, per)], rsbuf.at[me], rs_s.at[j], rs_r.at[me], "ctx", j)

    def w_rs(j):
        return remote(rsbuf.at[j], rsbuf.at[j], rs_s.at[j], rs_r.at[j], "ctx", j)

    def c_ag(j):
        return remote(agbuf.at[me], agbuf.at[me], ag_s.at[j], ag_r.at[me], "ctx", j)

    def w_ag(j):
        return remote(agbuf.at[j], agbuf.at[j], ag_s.at[j], ag_r.at[j], "ctx", j)

    def c_gn(j):
        return remote(gainbuf.at[me], gainbuf.at[me], gn_s.at[j], gn_r.at[me], "ctx", j)

    def w_gn(j):
        return remote(gainbuf.at[j], gainbuf.at[j], gn_s.at[j], gn_r.at[j], "ctx", j)

    reads = [
        pltpu.make_async_copy(src, dst, io_s.at[i])
        for i, (src, dst) in enumerate(
            ((stream_in, stream), (gout_in, gout), (query_in, query), (key_in, key))
        )
    ]
    for copy in reads:
        copy.start()
    writes = [
        pltpu.make_async_copy(src, dst, io_s.at[4 + i])
        for i, (src, dst) in enumerate(((inv_col, inv_out), (ss, sig_out), (ys, conv_out), (col, inner_out)))
    ]

    barrier = pltpu.get_barrier_semaphore()
    each(n, lambda j: j != me, lambda j: pl.semaphore_signal(
        barrier, inc=1, device_id={"ctx": j}, device_id_type=MESH))
    each(nch, lambda j: j != mc, lambda j: pl.semaphore_signal(
        barrier, inc=1, device_id={"ch": j}, device_id_type=MESH))

    for k in range(kt):
        mode_rows = pl.ds(k, MODES, stride=kt)
        res[mode_rows, :] = res_in[:, k * LANES : (k + 1) * LANES]
        lrate[mode_rows, :] = lrate_in[:, k * LANES : (k + 1) * LANES]
    rate = jnp.exp(lrate[...])
    apow[...] = jnp.exp(-rate)
    alen[...] = jnp.exp(-rate * float(rows))

    def lanes(k):
        return pl.ds(k * LANES, LANES)

    def rows_of(b):
        return pl.ds(pl.multiple_of(b * RB, RB), RB)

    def spread(b, k):
        return pl.ds(b * (RB * kt) + k, RB, stride=kt)

    def at(t):
        return pl.ds(pl.multiple_of(t * kt, kt), kt)

    def to_row(ref):
        return jnp.broadcast_to(jnp.sum(ref[...].T, axis=0, keepdims=True), (8, rows))

    def first(b, carry):
        r = rows_of(b)
        total = jnp.zeros((RB, LANES), F32)
        for k in range(kt):
            s = stream[r, lanes(k)].astype(F32)
            total += s * s
        col[r, :] = total
        return carry

    reads[0].wait()
    lax.fori_loop(0, nblk, first, 0)
    nrm_buf[mc] = to_row(col)
    pl.semaphore_wait(barrier, n - 1 + nch - 1)
    each(nch, lambda j: j != mc, lambda j: c_nrm(j).start())

    def cotangent(b, carry):
        r = rows_of(b)
        for k in range(kt):
            gs[spread(b, k), :] = gout[r, lanes(k)].astype(F32) * query[r, lanes(k)].astype(F32)
        return carry

    reads[1].wait()
    reads[2].wait()
    lax.fori_loop(0, nblk, cotangent, 0)

    def mode(ref, m):
        return ref[m * kt : (m + 1) * kt, :]

    def tree(terms):
        while len(terms) > 1:
            terms = [sum(terms[i + 1 : i + 2], terms[i]) for i in range(0, len(terms), 2)]
        return terms[0]

    def end_state(src, backward):
        a = [mode(apow, m) for m in range(MODES)]

        def body(i, carry):
            h = list(carry)
            for u in range(UNROLL):
                t = i * UNROLL + u
                x = src[at(rows - 1 - t if backward else t), :]
                for m in range(MODES):
                    h[m] = a[m] * h[m] + x
            return tuple(h)

        zero = jnp.zeros((kt, LANES), F32)
        return lax.fori_loop(0, nstep, body, (zero,) * MODES)

    ends = end_state(gs, True)
    for m in range(MODES):
        tbuf[me, m * kt : (m + 1) * kt, :] = ends[m]
    each(n, lambda j: j < me, lambda j: c_t(j).start())

    each(nch, lambda j: j != mc, lambda j: w_nrm(j).wait_recv())
    total = nrm_buf[0]
    for j in range(1, nch):
        total = total + nrm_buf[j]
    inv_row = lax.rsqrt(total / D + epsilon)
    inv_col[...] = jnp.broadcast_to(inv_row[0:1], (LANES, rows)).T
    writes[0].start()
    reads[3].wait()

    def second(b, carry):
        r = rows_of(b)
        iv = inv_col[r, :]
        for k in range(kt):
            normed = stream[r, lanes(k)].astype(F32) * iv * gain[k : k + 1, :]
            x = (key[r, lanes(k)].astype(F32) * normed).astype(jnp.bfloat16)
            xs[spread(b, k), :] = x.astype(F32)
        return carry

    lax.fori_loop(0, nblk, second, 0)
    ends = end_state(xs, False)
    for m in range(MODES):
        sbuf[me, m * kt : (m + 1) * kt, :] = ends[m]
    each(n, lambda j: j > me, lambda j: c_s(j).start())

    def backward(group):
        m0 = group * GROUP
        a = [mode(apow, m0 + m) for m in range(GROUP)]
        c = [mode(res, m0 + m) for m in range(GROUP)]

        def body(i, carry):
            q = list(carry)
            for u in range(UNROLL):
                t = rows - 1 - (i * UNROLL + u)
                g = gs[at(t), :]
                terms = [ss[at(t), :]] if group else []
                for m in range(GROUP):
                    q[m] = a[m] * q[m] + g
                    qbuf[t, m0 + m] = q[m]
                    terms.append(c[m] * q[m])
                ss[at(t), :] = tree(terms)
            return tuple(q)

        lax.fori_loop(0, nstep, body, tuple(mode(state.at[1], m0 + m) for m in range(GROUP)))

    def forward(group):
        m0 = group * GROUP
        a = [mode(apow, m0 + m) for m in range(GROUP)]
        c = [mode(res, m0 + m) for m in range(GROUP)]
        zero = jnp.zeros((kt, LANES), F32)

        def body(i, carry):
            h, gr, gw = (list(v) for v in carry)
            for u in range(UNROLL):
                t = i * UNROLL + u
                x = xs[at(t), :]
                g = gs[at(t), :]
                terms = [ys[at(t), :]] if group else []
                for m in range(GROUP):
                    z = a[m] * h[m]
                    gw[m] = gw[m] + z * qbuf[t, m0 + m]
                    h[m] = z + x
                    gr[m] = gr[m] + g * h[m]
                    terms.append(c[m] * h[m])
                ys[at(t), :] = tree(terms)
            return tuple(h), tuple(gr), tuple(gw)

        start = tuple(mode(state.at[0], m0 + m) for m in range(GROUP))
        unused, gr, gw = lax.fori_loop(0, nstep, body, (start, (zero,) * GROUP, (zero,) * GROUP))
        for m in range(GROUP):
            part[m0 + m] = gr[m]
            part[MODES + m0 + m] = gw[m]

    state[...] = jnp.zeros_like(state)

    def take_t(i):
        j = n - 1 - i
        w_t(j).wait_recv()
        state[1] = alen[...] * state[1] + tbuf[j]

    each(n, lambda i: n - 1 - i > me, take_t)
    for group in range(MODES // GROUP):
        backward(group)
    writes[1].start()

    def take_s(j):
        w_s(j).wait_recv()
        state[0] = alen[...] * state[0] + sbuf[j]

    each(n, lambda j: j < me, take_s)
    for group in range(MODES // GROUP):
        forward(group)
    writes[2].start()
    rsbuf[me] = part[pl.ds(me * per, per)]
    each(n, lambda j: j != me, lambda j: c_rs(j).start())

    def third(b, carry):
        r = rows_of(b)
        iv = inv_col[r, :]
        total = jnp.zeros((RB, LANES), F32)
        gains = list(carry)
        for k in range(kt):
            unit = stream[r, lanes(k)].astype(F32) * iv
            prod = ss[spread(b, k), :] * key[r, lanes(k)].astype(F32) * unit
            gains[k] = gains[k] + prod
            total += prod * gain[k : k + 1, :]
        col[r, :] = total
        return tuple(gains)

    gains = lax.fori_loop(0, nblk, third, (jnp.zeros((RB, LANES), F32),) * kt)
    inner_buf[mc] = to_row(col)
    each(nch, lambda j: j != mc, lambda j: c_inner(j).start())
    for k in range(kt):
        gainbuf[me, k : k + 1, :] = jnp.sum(gains[k], axis=0, keepdims=True)
    each(n, lambda j: j != me, lambda j: c_gn(j).start())

    each(n, lambda j: j != me, lambda j: w_rs(j).wait_recv())
    agbuf[me] = lax.fori_loop(1, n, lambda j, acc: acc + rsbuf[j], rsbuf[0])
    each(n, lambda j: j != me, lambda j: c_ag(j).start())

    each(nch, lambda j: j != mc, lambda j: w_inner(j).wait_recv())
    total = inner_buf[0]
    for j in range(1, nch):
        total = total + inner_buf[j]
    col[...] = jnp.broadcast_to((total / D)[0:1], (LANES, rows)).T
    writes[3].start()

    scale = 1.0 / math.sqrt(rows * n)
    each(n, lambda j: j != me, lambda j: w_gn(j).wait_recv())
    ggain[...] = lax.fori_loop(1, n, lambda j, acc: acc + gainbuf[j], gainbuf[0]) * scale
    each(n, lambda j: j != me, lambda j: w_ag(j).wait_recv())
    for m in range(2 * MODES):
        gmode[m * kt : (m + 1) * kt, :] = agbuf[m // per, m % per] * scale

    each(nch, lambda j: j != mc, lambda j: c_nrm(j).wait_send())
    each(nch, lambda j: j != mc, lambda j: c_inner(j).wait_send())
    each(n, lambda j: j < me, lambda j: c_t(j).wait_send())
    each(n, lambda j: j > me, lambda j: c_s(j).wait_send())
    each(n, lambda j: j != me, lambda j: c_gn(j).wait_send())
    each(n, lambda j: j != me, lambda j: c_rs(j).wait_send())
    each(n, lambda j: j != me, lambda j: c_ag(j).wait_send())
    for copy in writes:
        copy.wait()


def finish(
    kt,
    stream, key, query, gout, conv, sig, inv, inner, gain, res, lrate, ggain_in, gmode,
    out, gstream, gkey, gquery, ggain, gres, grate,
):
    @pl.when(pl.program_id(0) == 0)
    def _():
        ggain[...] = ggain_in[...]
        for k in range(kt):
            cols = slice(k * LANES, (k + 1) * LANES)
            gres[:, cols] = gmode[pl.ds(k, MODES, stride=kt), :]
            weighted = gmode[pl.ds(MODES * kt + k, MODES, stride=kt), :]
            grate[:, cols] = -jnp.exp(lrate[:, cols]) * res[:, cols] * weighted

    def body(b, carry):
        r = pl.ds(pl.multiple_of(b * RB, RB), RB)
        iv = inv[r, :]
        mean = inner[r, :]
        for k in range(kt):
            cols = pl.ds(k * LANES, LANES)
            spread = pl.ds(b * (RB * kt) + k, RB, stride=kt)
            gk = gain[k : k + 1, :]
            conv_k = conv[spread, :]
            sig_k = sig[spread, :]
            unit = stream[r, cols].astype(F32) * iv
            out[r, cols] = (query[r, cols].astype(F32) * conv_k).astype(jnp.bfloat16)
            gquery[r, cols] = (gout[r, cols].astype(F32) * conv_k).astype(jnp.bfloat16)
            gkey[r, cols] = (sig_k * (unit * gk)).astype(jnp.bfloat16)
            unit_grad = sig_k * key[r, cols].astype(F32) * gk
            gstream[r, cols] = (iv * (unit_grad - unit * mean)).astype(jnp.bfloat16)
        return carry

    lax.fori_loop(0, stream.shape[0] // RB, body, 0)


def local(n, nch, stream, key_gate, query_gate, grad_output, norm_gain, residue, log_rate):
    rows, channels = stream.shape
    kt = channels // LANES
    per = 2 * MODES // n
    vm = pl.BlockSpec(memory_space=pltpu.VMEM)
    anywhere = pl.BlockSpec(memory_space=pl.ANY)
    wide = jax.ShapeDtypeStruct((rows, channels), jnp.bfloat16)
    flat_out = jax.ShapeDtypeStruct((rows * kt, LANES), F32)
    one_out = jax.ShapeDtypeStruct((rows, LANES), F32)
    gain_out = jax.ShapeDtypeStruct((kt, LANES), F32)
    mode_out = jax.ShapeDtypeStruct((2 * MODES * kt, LANES), F32)
    dma = pltpu.SemaphoreType.DMA
    held = pltpu.VMEM((rows, channels), jnp.bfloat16)
    flat = pltpu.VMEM((rows * kt, LANES), F32)
    one = pltpu.VMEM((rows, LANES), F32)
    lined = pltpu.VMEM((nch, 8, rows), F32)
    ends = pltpu.VMEM((n, MODES * kt, LANES), F32)
    modal = pltpu.VMEM((MODES * kt, LANES), F32)
    pieces = pltpu.VMEM((n, per, kt, LANES), F32)
    gain = norm_gain.reshape(kt, LANES)
    res, lrate = residue.T, log_rate.T
    conv, sig, inv, inner, ggain, gmode = pl.pallas_call(
        functools.partial(kernel, n, nch, rows, kt),
        out_shape=(flat_out, flat_out, one_out, one_out, gain_out, mode_out),
        in_specs=[anywhere] * 4 + [vm] * 3,
        out_specs=(anywhere,) * 4 + (vm,) * 2,
        scratch_shapes=[
            held, held, held, held,
            flat, flat, flat, flat,
            pltpu.VMEM((rows, MODES, kt, LANES), F32),
            modal, modal, modal, modal, one, one,
            lined, lined, dma((8,)), ends, ends,
            pltpu.VMEM((2, MODES * kt, LANES), F32),
            pltpu.VMEM((2 * MODES, kt, LANES), F32),
            pieces, pieces,
            pltpu.VMEM((n, kt, LANES), F32),
            dma((nch,)), dma((nch,)), dma((nch,)), dma((nch,)),
        ] + [dma((n,))] * 10,
        compiler_params=pltpu.CompilerParams(
            collective_id=0, has_side_effects=True, vmem_limit_bytes=56 * 2**20
        ),
    )(stream, key_gate, query_gate, grad_output, gain, res, lrate)

    step = min(rows, 64)
    wide_spec = pl.BlockSpec((step, channels), lambda i: (i, 0))
    flat_spec = pl.BlockSpec((step * kt, LANES), lambda i: (i, 0))
    one_spec = pl.BlockSpec((step, LANES), lambda i: (i, 0))
    whole = lambda *shape: pl.BlockSpec(shape, lambda i: (0, 0))
    mode_spec = whole(MODES, channels)
    gain_spec = whole(kt, LANES)
    mode_t = jax.ShapeDtypeStruct((MODES, channels), F32)
    out, gstream, gkey, gquery, ggain, gres, grate = pl.pallas_call(
        functools.partial(finish, kt),
        grid=(rows // step,),
        out_shape=(wide, wide, wide, wide, gain_out, mode_t, mode_t),
        in_specs=[wide_spec] * 4 + [flat_spec] * 2 + [one_spec] * 2
        + [gain_spec, mode_spec, mode_spec, gain_spec, whole(2 * MODES * kt, LANES)],
        out_specs=(wide_spec,) * 4 + (gain_spec, mode_spec, mode_spec),
        compiler_params=pltpu.CompilerParams(vmem_limit_bytes=56 * 2**20),
    )(stream, key_gate, query_gate, grad_output, conv, sig, inv, inner, gain, res, lrate, ggain, gmode)
    return out, gstream, gkey, gquery, ggain.reshape(channels), gres.T, grate.T


def solution(mesh):
    wide = P("ctx", "ch")
    thin = P("ch", None)
    return jax.shard_map(
        functools.partial(local, mesh.shape["ctx"], mesh.shape["ch"]),
        mesh=mesh,
        in_specs=(wide, wide, wide, wide, P("ch"), thin, thin),
        out_specs=(wide, wide, wide, wide, P("ch"), thin, thin),
        check_vma=False,
    )
```

time: 59 us -> 51.6 us (0.87)
  local copies, waits for them, and re-layouts: 10.8 us -> 0 us
  Pallas kernels: 47.1 us -> 50.7 us
    unnamed x17 -> x0, local copies, waits for them, and re-layouts: 9.29 us -> none
    pallas_call x1 -> x2, Pallas kernels: 47.1 us -> 50.7 us  [the longest x1 42.1 us: local(): pl.pallas_call(functools.partial(kernel, n, nch, rows, kt), out_shape=(fl...]
    transpose x1 -> x0, local copies, waits for them, and re-layouts: 1.54 us -> none  [local(): grate.reshape(MODES, channels)]
where the time goes in v1:
time: 51.6 us; the launch traced here: 51.3 us
  Pallas kernels  50.7 us (98%)
  between operations  0.64 us (1%)
    pallas_call x1, Pallas kernels, local(): pl.pallas_call(functools.partial(kernel, n, nch, rows, kt), out_shape=(fl...  42.1 us
    pallas_call x1, Pallas kernels, local(): pl.pallas_call(functools.partial(finish, kt), grid=(rows // step,), out_s...  8.54 us

profile of v1, /device:TPU:0, one launch (start us, length us, event | category | flops | bytes accessed | tf_op | source)
XLA Modules:
  0.0 51.3 jit_solution(9846498094238261944)
XLA Ops:
  0.6 42.1 %shard_map.126 = (f32[4096,128]{1,0:T(8,128)}, f32[4096,128]{1,0:T(8,128)}, f32[512,128]{1,0:T(8,128)}, f32[512,128]{1,0:T(8,128)}, f32[8,128]{1,0:T(8,128)}, /*index=5*/f32[256,128]{1,0:T(8,128)}) custom-call(bf16[512,1024]{1,0:T(8,128)(2,1)} %stream.1, bf16[512,1024]{1,0:T(8,128)(2,1)} %key.1, bf16[512,1024]{1,0:T(8,128)(2,1)} %query.1, ...), custom_call_target="tpu_custom_call" | custom-call | tf_op jit(solution)/shard_map/pallas_call | solution.py:390
  42.8 8.5 %shard_map.127 = (bf16[512,1024]{1,0:T(8,128)(2,1)}, bf16[512,1024]{1,0:T(8,128)(2,1)}, bf16[512,1024]{1,0:T(8,128)(2,1)}, bf16[512,1024]{1,0:T(8,128)(2,1)}, f3...) custom-call(bf16[512,1024]{1,0:T(8,128)(2,1)} %stream.1, bf16[512,1024]{1,0:T(8,128)(2,1)} %key.1, ...), custom_call_target="tpu_custom_call" | custom-call | tf_op jit(solution)/shard_map/pallas_call | solution.py:420

commit v2 on v1

--- a/solution.py
+++ b/solution.py
@@ -15,6 +15,7 @@
 RB = 16
 UNROLL = 8
 GROUP = 8
+PAD = 1
 MESH = pl.DeviceIdType.MESH
 F32 = jnp.float32
 
@@ -33,6 +34,7 @@
     nblk = rows // RB
     nstep = rows // UNROLL
     per = 2 * MODES // n
+    ps = kt + PAD
 
     def each(count, test, fn):
         def body(j, carry):
@@ -126,10 +128,10 @@
         return pl.ds(pl.multiple_of(b * RB, RB), RB)
 
     def spread(b, k):
-        return pl.ds(b * (RB * kt) + k, RB, stride=kt)
+        return pl.ds(b * (RB * ps) + k, RB, stride=ps)
 
     def at(t):
-        return pl.ds(pl.multiple_of(t * kt, kt), kt)
+        return pl.ds(t * ps, kt)
 
     def to_row(ref):
         return jnp.broadcast_to(jnp.sum(ref[...].T, axis=0, keepdims=True), (8, rows))
@@ -345,13 +347,15 @@
             weighted = gmode[pl.ds(MODES * kt + k, MODES, stride=kt), :]
             grate[:, cols] = -jnp.exp(lrate[:, cols]) * res[:, cols] * weighted
 
+    ps = kt + PAD
+
     def body(b, carry):
         r = pl.ds(pl.multiple_of(b * RB, RB), RB)
         iv = inv[r, :]
         mean = inner[r, :]
         for k in range(kt):
             cols = pl.ds(k * LANES, LANES)
-            spread = pl.ds(b * (RB * kt) + k, RB, stride=kt)
+            spread = pl.ds(b * (RB * ps) + k, RB, stride=ps)
             gk = gain[k : k + 1, :]
             conv_k = conv[spread, :]
             sig_k = sig[spread, :]
@@ -373,13 +377,13 @@
     vm = pl.BlockSpec(memory_space=pltpu.VMEM)
     anywhere = pl.BlockSpec(memory_space=pl.ANY)
     wide = jax.ShapeDtypeStruct((rows, channels), jnp.bfloat16)
-    flat_out = jax.ShapeDtypeStruct((rows * kt, LANES), F32)
+    flat_out = jax.ShapeDtypeStruct((rows * (kt + PAD), LANES), F32)
     one_out = jax.ShapeDtypeStruct((rows, LANES), F32)
     gain_out = jax.ShapeDtypeStruct((kt, LANES), F32)
     mode_out = jax.ShapeDtypeStruct((2 * MODES * kt, LANES), F32)
     dma = pltpu.SemaphoreType.DMA
     held = pltpu.VMEM((rows, channels), jnp.bfloat16)
-    flat = pltpu.VMEM((rows * kt, LANES), F32)
+    flat = pltpu.VMEM((rows * (kt + PAD), LANES), F32)
     one = pltpu.VMEM((rows, LANES), F32)
     lined = pltpu.VMEM((nch, 8, rows), F32)
     ends = pltpu.VMEM((n, MODES * kt, LANES), F32)
@@ -411,7 +415,7 @@
 
     step = min(rows, 64)
     wide_spec = pl.BlockSpec((step, channels), lambda i: (i, 0))
-    flat_spec = pl.BlockSpec((step * kt, LANES), lambda i: (i, 0))
+    flat_spec = pl.BlockSpec((step * (kt + PAD), LANES), lambda i: (i, 0))
     one_spec = pl.BlockSpec((step, LANES), lambda i: (i, 0))
     whole = lambda *shape: pl.BlockSpec(shape, lambda i: (0, 0))
     mode_spec = whole(MODES, channels)

time: 51.6 us -> 51.7 us (level)
  no operation moved by 1% of the time
where the time goes in v2:
time: 51.7 us; the launch traced here: 51.4 us
  Pallas kernels  50.7 us (98%)
  between operations  0.64 us (1%)
    pallas_call x1, Pallas kernels, local(): pl.pallas_call(functools.partial(kernel, n, nch, rows, kt), out_shape=(fl...  42.2 us
    pallas_call x1, Pallas kernels, local(): pl.pallas_call(functools.partial(finish, kt), grid=(rows // step,), out_s...  8.53 us

profile of v2, /device:TPU:0, one launch (start us, length us, event | category | flops | bytes accessed | tf_op | source)
XLA Modules:
  0.0 51.4 jit_solution(3302282826168567141)
XLA Ops:
  0.6 42.2 %shard_map.126 = (f32[4608,128]{1,0:T(8,128)}, f32[4608,128]{1,0:T(8,128)}, f32[512,128]{1,0:T(8,128)}, f32[512,128]{1,0:T(8,128)}, f32[8,128]{1,0:T(8,128)}, /*index=5*/f32[256,128]{1,0:T(8,128)}) custom-call(bf16[512,1024]{1,0:T(8,128)(2,1)} %stream.1, bf16[512,1024]{1,0:T(8,128)(2,1)} %key.1, bf16[512,1024]{1,0:T(8,128)(2,1)} %query.1, ...), custom_call_target="tpu_custom_call" | custom-call | tf_op jit(solution)/shard_map/pallas_call | solution.py:394
  42.8 8.5 %shard_map.127 = (bf16[512,1024]{1,0:T(8,128)(2,1)}, bf16[512,1024]{1,0:T(8,128)(2,1)}, bf16[512,1024]{1,0:T(8,128)(2,1)}, bf16[512,1024]{1,0:T(8,128)(2,1)}, f3...) custom-call(bf16[512,1024]{1,0:T(8,128)(2,1)} %stream.1, bf16[512,1024]{1,0:T(8,128)(2,1)} %key.1, ...), custom_call_target="tpu_custom_call" | custom-call | tf_op jit(solution)/shard_map/pallas_call | solution.py:424

commit v3 on v1

--- a/solution.py
+++ b/solution.py
@@ -22,8 +22,8 @@
 def kernel(
     n, nch, rows, kt,
     stream_in, key_in, query_in, gout_in, gain, res_in, lrate_in,
-    conv_out, sig_out, inv_out, inner_out, ggain, gmode,
-    stream, key, query, gout, xs, gs, ys, ss, qbuf, res, lrate, apow, alen,
+    out_out, gstream_out, gkey_out, gquery_out, ggain, gmode,
+    stream, key, query, gout, out, gstream, gkey, gquery, xs, gs, ys, ss, qbuf, res, lrate, apow, alen,
     col, inv_col, nrm_buf, inner_buf, io_s,
     sbuf, tbuf, state, part, rsbuf, agbuf, gainbuf,
     nrm_s, nrm_r, inner_s, inner_r, s_s, s_r, t_s, t_r, rs_s, rs_r, ag_s, ag_r, gn_s, gn_r,
@@ -102,7 +102,7 @@
         copy.start()
     writes = [
         pltpu.make_async_copy(src, dst, io_s.at[4 + i])
-        for i, (src, dst) in enumerate(((inv_col, inv_out), (ss, sig_out), (ys, conv_out), (col, inner_out)))
+        for i, (src, dst) in enumerate(((gkey, gkey_out), (out, out_out), (gquery, gquery_out), (gstream, gstream_out)))
     ]
 
     barrier = pltpu.get_barrier_semaphore()
@@ -193,7 +193,6 @@
         total = total + nrm_buf[j]
     inv_row = lax.rsqrt(total / D + epsilon)
     inv_col[...] = jnp.broadcast_to(inv_row[0:1], (LANES, rows)).T
-    writes[0].start()
     reads[3].wait()
 
     def second(b, carry):
@@ -269,7 +268,6 @@
     each(n, lambda i: n - 1 - i > me, take_t)
     for group in range(MODES // GROUP):
         backward(group)
-    writes[1].start()
 
     def take_s(j):
         w_s(j).wait_recv()
@@ -278,7 +276,6 @@
     each(n, lambda j: j < me, take_s)
     for group in range(MODES // GROUP):
         forward(group)
-    writes[2].start()
     rsbuf[me] = part[pl.ds(me * per, per)]
     each(n, lambda j: j != me, lambda j: c_rs(j).start())
 
@@ -289,9 +286,12 @@
         gains = list(carry)
         for k in range(kt):
             unit = stream[r, lanes(k)].astype(F32) * iv
-            prod = ss[spread(b, k), :] * key[r, lanes(k)].astype(F32) * unit
+            sig = ss[spread(b, k), :]
+            gk = gain[k : k + 1, :]
+            gkey[r, lanes(k)] = (sig * (unit * gk)).astype(jnp.bfloat16)
+            prod = sig * key[r, lanes(k)].astype(F32) * unit
             gains[k] = gains[k] + prod
-            total += prod * gain[k : k + 1, :]
+            total += prod * gk
         col[r, :] = total
         return tuple(gains)
 
@@ -301,16 +301,41 @@
     for k in range(kt):
         gainbuf[me, k : k + 1, :] = jnp.sum(gains[k], axis=0, keepdims=True)
     each(n, lambda j: j != me, lambda j: c_gn(j).start())
+    writes[0].start()
 
     each(n, lambda j: j != me, lambda j: w_rs(j).wait_recv())
     agbuf[me] = lax.fori_loop(1, n, lambda j, acc: acc + rsbuf[j], rsbuf[0])
     each(n, lambda j: j != me, lambda j: c_ag(j).start())
+
+    def fourth(b, carry):
+        r = rows_of(b)
+        for k in range(kt):
+            conv = ys[spread(b, k), :]
+            out[r, lanes(k)] = (query[r, lanes(k)].astype(F32) * conv).astype(jnp.bfloat16)
+            gquery[r, lanes(k)] = (gout[r, lanes(k)].astype(F32) * conv).astype(jnp.bfloat16)
+        return carry
+
+    lax.fori_loop(0, nblk, fourth, 0)
+    writes[1].start()
+    writes[2].start()
 
     each(nch, lambda j: j != mc, lambda j: w_inner(j).wait_recv())
     total = inner_buf[0]
     for j in range(1, nch):
         total = total + inner_buf[j]
     col[...] = jnp.broadcast_to((total / D)[0:1], (LANES, rows)).T
+
+    def fifth(b, carry):
+        r = rows_of(b)
+        iv = inv_col[r, :]
+        mean = col[r, :]
+        for k in range(kt):
+            unit = stream[r, lanes(k)].astype(F32) * iv
+            unit_grad = ss[spread(b, k), :] * key[r, lanes(k)].astype(F32) * gain[k : k + 1, :]
+            gstream[r, lanes(k)] = (iv * (unit_grad - unit * mean)).astype(jnp.bfloat16)
+        return carry
+
+    lax.fori_loop(0, nblk, fifth, 0)
     writes[3].start()
 
     scale = 1.0 / math.sqrt(rows * n)
@@ -332,38 +357,36 @@
 
 
 def finish(
-    kt,
-    stream, key, query, gout, conv, sig, inv, inner, gain, res, lrate, ggain_in, gmode,
-    out, gstream, gkey, gquery, ggain, gres, grate,
+    kt, parts,
+    a_in, b_in, c_in, d_in, res, lrate, ggain_in, gmode,
+    a_out, b_out, c_out, d_out, ggain, gres, grate,
+    a, b, c, d, read_s, write_s,
 ):
-    @pl.when(pl.program_id(0) == 0)
-    def _():
-        ggain[...] = ggain_in[...]
-        for k in range(kt):
-            cols = slice(k * LANES, (k + 1) * LANES)
-            gres[:, cols] = gmode[pl.ds(k, MODES, stride=kt), :]
-            weighted = gmode[pl.ds(MODES * kt + k, MODES, stride=kt), :]
-            grate[:, cols] = -jnp.exp(lrate[:, cols]) * res[:, cols] * weighted
-
-    def body(b, carry):
-        r = pl.ds(pl.multiple_of(b * RB, RB), RB)
-        iv = inv[r, :]
-        mean = inner[r, :]
-        for k in range(kt):
-            cols = pl.ds(k * LANES, LANES)
-            spread = pl.ds(b * (RB * kt) + k, RB, stride=kt)
-            gk = gain[k : k + 1, :]
-            conv_k = conv[spread, :]
-            sig_k = sig[spread, :]
-            unit = stream[r, cols].astype(F32) * iv
-            out[r, cols] = (query[r, cols].astype(F32) * conv_k).astype(jnp.bfloat16)
-            gquery[r, cols] = (gout[r, cols].astype(F32) * conv_k).astype(jnp.bfloat16)
-            gkey[r, cols] = (sig_k * (unit * gk)).astype(jnp.bfloat16)
-            unit_grad = sig_k * key[r, cols].astype(F32) * gk
-            gstream[r, cols] = (iv * (unit_grad - unit * mean)).astype(jnp.bfloat16)
-        return carry
-
-    lax.fori_loop(0, stream.shape[0] // RB, body, 0)
+    height = a.shape[0] // parts
+    moves = []
+    for i in range(parts):
+        r = pl.ds(i * height, height)
+        for j, (src, held, dst) in enumerate(
+            ((a_in, a, a_out), (b_in, b, b_out), (c_in, c, c_out), (d_in, d, d_out))
+        ):
+            at = i * 4 + j
+            moves.append((
+                pltpu.make_async_copy(src.at[r], held.at[r], read_s.at[at]),
+                pltpu.make_async_copy(held.at[r], dst.at[r], write_s.at[at]),
+            ))
+    for read, write in moves:
+        read.start()
+    ggain[...] = ggain_in[...]
+    for k in range(kt):
+        cols = slice(k * LANES, (k + 1) * LANES)
+        gres[:, cols] = gmode[pl.ds(k, MODES, stride=kt), :]
+        weighted = gmode[pl.ds(MODES * kt + k, MODES, stride=kt), :]
+        grate[:, cols] = -jnp.exp(lrate[:, cols]) * res[:, cols] * weighted
+    for read, write in moves:
+        read.wait()
+        write.start()
+    for read, write in moves:
+        write.wait()
 
 
 def local(n, nch, stream, key_gate, query_gate, grad_output, norm_gain, residue, log_rate):
@@ -373,8 +396,6 @@
     vm = pl.BlockSpec(memory_space=pltpu.VMEM)
     anywhere = pl.BlockSpec(memory_space=pl.ANY)
     wide = jax.ShapeDtypeStruct((rows, channels), jnp.bfloat16)
-    flat_out = jax.ShapeDtypeStruct((rows * kt, LANES), F32)
-    one_out = jax.ShapeDtypeStruct((rows, LANES), F32)
     gain_out = jax.ShapeDtypeStruct((kt, LANES), F32)
     mode_out = jax.ShapeDtypeStruct((2 * MODES * kt, LANES), F32)
     dma = pltpu.SemaphoreType.DMA
@@ -387,13 +408,13 @@
     pieces = pltpu.VMEM((n, per, kt, LANES), F32)
     gain = norm_gain.reshape(kt, LANES)
     res, lrate = residue.T, log_rate.T
-    conv, sig, inv, inner, ggain, gmode = pl.pallas_call(
+    out, gstream, gkey, gquery, ggain, gmode = pl.pallas_call(
         functools.partial(kernel, n, nch, rows, kt),
-        out_shape=(flat_out, flat_out, one_out, one_out, gain_out, mode_out),
+        out_shape=(wide, wide, wide, wide, gain_out, mode_out),
         in_specs=[anywhere] * 4 + [vm] * 3,
         out_specs=(anywhere,) * 4 + (vm,) * 2,
         scratch_shapes=[
-            held, held, held, held,
+            held, held, held, held, held, held, held, held,
             flat, flat, flat, flat,
             pltpu.VMEM((rows, MODES, kt, LANES), F32),
             modal, modal, modal, modal, one, one,
@@ -409,23 +430,16 @@
         ),
     )(stream, key_gate, query_gate, grad_output, gain, res, lrate)
 
-    step = min(rows, 64)
-    wide_spec = pl.BlockSpec((step, channels), lambda i: (i, 0))
-    flat_spec = pl.BlockSpec((step * kt, LANES), lambda i: (i, 0))
-    one_spec = pl.BlockSpec((step, LANES), lambda i: (i, 0))
-    whole = lambda *shape: pl.BlockSpec(shape, lambda i: (0, 0))
-    mode_spec = whole(MODES, channels)
-    gain_spec = whole(kt, LANES)
+    parts = 4
     mode_t = jax.ShapeDtypeStruct((MODES, channels), F32)
     out, gstream, gkey, gquery, ggain, gres, grate = pl.pallas_call(
-        functools.partial(finish, kt),
-        grid=(rows // step,),
+        functools.partial(finish, kt, parts),
         out_shape=(wide, wide, wide, wide, gain_out, mode_t, mode_t),
-        in_specs=[wide_spec] * 4 + [flat_spec] * 2 + [one_spec] * 2
-        + [gain_spec, mode_spec, mode_spec, gain_spec, whole(2 * MODES * kt, LANES)],
-        out_specs=(wide_spec,) * 4 + (gain_spec, mode_spec, mode_spec),
+        in_specs=[anywhere] * 4 + [vm] * 4,
+        out_specs=(anywhere,) * 4 + (vm,) * 3,
+        scratch_shapes=[held, held, held, held, dma((4 * parts,)), dma((4 * parts,))],
         compiler_params=pltpu.CompilerParams(vmem_limit_bytes=56 * 2**20),
-    )(stream, key_gate, query_gate, grad_output, conv, sig, inv, inner, gain, res, lrate, ggain, gmode)
+    )(out, gstream, gkey, gquery, res, lrate, ggain, gmode)
     return out, gstream, gkey, gquery, ggain.reshape(channels), gres.T, grate.T
 
 

time: 51.6 us -> 48.4 us (0.938)
  Pallas kernels: 50.7 us -> 47.5 us
    pallas_call x2, Pallas kernels: 50.7 us -> 47.5 us  [the longest x1 42 us: local(): pl.pallas_call(functools.partial(kernel, n, nch, rows, kt), out_shape=(wi...]
where the time goes in v3:
time: 48.4 us; the launch traced here: 48.2 us
  Pallas kernels  47.5 us (98%)
  between operations  0.64 us (1%)
    pallas_call x1, Pallas kernels, local(): pl.pallas_call(functools.partial(kernel, n, nch, rows, kt), out_shape=(wi...  42 us
    pallas_call x1, Pallas kernels, local(): pl.pallas_call(functools.partial(finish, kt, parts), out_shape=(wide, wid...  5.49 us

profile of v3, /device:TPU:0, one launch (start us, length us, event | category | flops | bytes accessed | tf_op | source)
XLA Modules:
  0.0 48.2 jit_solution(9579652152798323059)
XLA Ops:
  0.6 42.0 %shard_map.126 = (bf16[512,1024]{1,0:T(8,128)(2,1)}, bf16[512,1024]{1,0:T(8,128)(2,1)}, bf16[512,1024]{1,0:T(8,128)(2,1)}, bf16[512,1024]{1,0:T(8,128)(2,1)}, f32[8,128]{1,0:T(8,128)}, /*index=5*/f32[256,128]{1,0:T(8,128)}) custom-call(bf16[512,1024]{1,0:T(8,128)(2,1)} %stream_in.1, bf16[512,1024]{1,0:T(8,128)(2,1)} %key_in.1, bf16[512,1024]{1,0:T(8,128)(2,1)} %query_in.1, ...), custom_call_target="tpu_custom_call" | custom-call | tf_op jit(solution)/shard_map/pallas_call | solution.py:411
  42.7 5.5 %shard_map.127 = (bf16[512,1024]{1,0:T(8,128)(2,1)}, bf16[512,1024]{1,0:T(8,128)(2,1)}, bf16[512,1024]{1,0:T(8,128)(2,1)}, bf16[512,1024]{1,0:T(8,128)(2,1)}, f3...) custom-call(bf16[512,1024]{1,0:T(8,128)(2,1)} %get-tuple-element.20.a_in, ...), custom_call_target="tpu_custom_call" | custom-call | tf_op jit(solution)/shard_map/pallas_call | solution.py:435

commit v4 on v3

--- a/solution.py
+++ b/solution.py
@@ -13,7 +13,7 @@
 epsilon = 1e-05
 LANES = 128
 RB = 16
-UNROLL = 8
+UNROLL = 16
 GROUP = 8
 MESH = pl.DeviceIdType.MESH
 F32 = jnp.float32

time: 48.4 us -> 47.7 us (0.986)
  Pallas kernels: 47.5 us -> 46.9 us
    pallas_call x1, Pallas kernels: 42 us -> 41.4 us  [local(): pl.pallas_call(functools.partial(kernel, n, nch, rows, kt), out_shape=(wi...]
where the time goes in v4:
time: 47.7 us; the launch traced here: 47.5 us
  Pallas kernels  46.9 us (98%)
  between operations  0.64 us (1%)
    pallas_call x1, Pallas kernels, local(): pl.pallas_call(functools.partial(kernel, n, nch, rows, kt), out_shape=(wi...  41.4 us
    pallas_call x1, Pallas kernels, local(): pl.pallas_call(functools.partial(finish, kt, parts), out_shape=(wide, wid...  5.49 us

profile of v4, /device:TPU:0, one launch (start us, length us, event | category | flops | bytes accessed | tf_op | source)
XLA Modules:
  0.0 47.5 jit_solution(15329539563606988232)
XLA Ops:
  0.6 41.4 %shard_map.126 = (bf16[512,1024]{1,0:T(8,128)(2,1)}, bf16[512,1024]{1,0:T(8,128)(2,1)}, bf16[512,1024]{1,0:T(8,128)(2,1)}, bf16[512,1024]{1,0:T(8,128)(2,1)}, f32[8,128]{1,0:T(8,128)}, /*index=5*/f32[256,128]{1,0:T(8,128)}) custom-call(bf16[512,1024]{1,0:T(8,128)(2,1)} %stream_in.1, bf16[512,1024]{1,0:T(8,128)(2,1)} %key_in.1, bf16[512,1024]{1,0:T(8,128)(2,1)} %query_in.1, ...), custom_call_target="tpu_custom_call" | custom-call | tf_op jit(solution)/shard_map/pallas_call | solution.py:411
  42.0 5.5 %shard_map.127 = (bf16[512,1024]{1,0:T(8,128)(2,1)}, bf16[512,1024]{1,0:T(8,128)(2,1)}, bf16[512,1024]{1,0:T(8,128)(2,1)}, bf16[512,1024]{1,0:T(8,128)(2,1)}, f3...) custom-call(bf16[512,1024]{1,0:T(8,128)(2,1)} %get-tuple-element.20.a_in, ...), custom_call_target="tpu_custom_call" | custom-call | tf_op jit(solution)/shard_map/pallas_call | solution.py:435
